TPU v7x, 32 devices: a whole 2x2x4 slice. The times are simulated.
32 devices in a mesh: mp: 4 (over y, x), fsdp: 8 (over z, core).
Axes of the slice: x: 2, y: 2, z: 4, core: 2. Of those that a mesh axis runs over, the one named last changes fastest.
Arguments:
- weights: bfloat16 [4, 4096, 14336], P('mp', None, 'fsdp'), may hold values from -6 to 6
- acts: bfloat16 [4, 1024, 4096], P('mp', 'fsdp'), may hold values from -6 to 6
- cotangent: bfloat16 [4, 1024, 14336], P('mp', 'fsdp'), may hold values from -0.26367188 to 0.26367188
- token_ids: int32 [4, 1024], P('mp', 'fsdp'), may hold values from 0 to 31999, as said below
Outputs:
- merged: bfloat16 [4096, 14336], P('mp', 'fsdp')
Inputs may be any that keep to these rules, and one draw needn't show every extreme that they name: `token_ids`: each calibration sequence of 512 tokens holds live ids of 1 to 31999 first and then padding ids 0, at most 256 of them.
All inputs are finite; a program needn't handle non-finite values.
Results may differ from a plain program's by a relative error of at most 0.001.
Values may be sent and summed in bfloat16 or wider, within the bound.
A program may use at most 192 MiB of HBM per device.

v0:
```python
import jax
import jax.numpy as jnp
from jax import lax
from jax.sharding import PartitionSpec as P

SEQS = 2


damping = 0.1


def sequence_fisher(acts_cols, grads_cols):
    token_count, row_count = acts_cols.shape
    acts_split = acts_cols.reshape(SEQS, token_count // SEQS, row_count)
    grads_split = grads_cols.reshape(SEQS, token_count // SEQS, grads_cols.shape[1])
    grads = jnp.einsum("str,stf->srf", acts_split, grads_split, preferred_element_type=jnp.float32)
    return jnp.sum(grads * grads, axis=0) / SEQS + damping


def per_device(weights, acts, cotangent, token_ids):
    live_rows = (token_ids[0] > 0).astype(jnp.bfloat16)
    masked = cotangent[0] * live_rows[:, None]
    columns = lax.all_to_all(masked, "fsdp", split_axis=1, concat_axis=0, tiled=True)
    acts_blocks = lax.all_to_all(acts, "mp", split_axis=2, concat_axis=0, tiled=True)
    acts_models = lax.all_gather(acts_blocks, "fsdp", axis=1, tiled=True)
    weight_models = lax.all_to_all(weights, "mp", split_axis=1, concat_axis=0, tiled=True)
    grads_models = lax.all_gather(columns[None], "mp", axis=0, tiled=True)

    def add_model(totals, inputs):
        numerator, denominator = totals
        model_acts, model_grads, model_weights = inputs
        importance = sequence_fisher(model_acts, model_grads)
        return (
            (numerator + importance * model_weights.astype(jnp.float32), denominator + importance),
            None,
        )

    shape = weight_models.shape[1:]
    start = (jnp.zeros(shape, jnp.float32), jnp.zeros(shape, jnp.float32))
    (numerator, denominator), _ = lax.scan(
        add_model, start, (acts_models, grads_models, weight_models)
    )
    return (numerator / denominator).astype(jnp.bfloat16)


def solution(mesh):
    return jax.shard_map(
        per_device,
        mesh=mesh,
        in_specs=(
            P("mp", None, "fsdp"),
            P("mp", "fsdp", None),
            P("mp", "fsdp", None),
            P("mp", "fsdp"),
        ),
        out_specs=P("mp", "fsdp"),
        check_vma=False,
    )
```

profile of v0, /device:TPU:0, one launch (start us, length us, event | category | flops | bytes accessed | tf_op | source)
XLA Modules:
  0.0 744.7 jit_solution(2436945090940071446)
XLA Ops:
  6.5 0.0 all-gather.6.cloned.1.call-start
  6.5 5.0 copy.16
  11.6 0.5 broadcast.39
  12.1 22.4 %reduce = bf16[4096,128]{1,0:T(8,128)(2,1)S(1)} reduce(bf16[4096,1,128]{2,1,0:T(2,128)(2,1)S(1)} %bitcast.43, bf16[]{:T(256)} %broadcast.39), dimensions={1}, to_apply=%bitcast.18.reduce_sub_computation | reduce | bytes 2097154
  34.5 0.3 reshape.39
  34.8 19.1 %all_to_all.43 = bf16[4,2,65536]{2,1,0:T(2,128)(2,1)S(1)} all-to-all(bf16[4,2,65536]{2,1,0:T(2,128)(2,1)S(1)} %reshape.39), channel_id=1, replica_groups=mesh['mp'=4,'fsdp'=8] {'mp'}, dimensions={0} | all-to-all | bytes 2097152 | tf_op jit(solution)/shard_map/all_to_all | solution.py:24
  53.9 0.0 copy-start.1
  53.9 0.9 reshape.40
  54.9 1.1 copy.22
  56.0 0.0 all-gather.6.cloned.1.call-update
  56.0 0.0 all-gather.4.cloned.1.call-start
  56.1 2.8 copy.24
  58.9 0.0 copy-done.1
  58.9 1.2 copy_multiply_fusion
  60.1 154.4 %all_to_all.44 = bf16[128,8,1792]{2,0,1:T(8,128)(2,1)} all-to-all(bf16[128,8,1792]{2,0,1:T(8,128)(2,1)S(1)} %copy_multiply_fusion), channel_id=1, replica_groups=mesh['mp'=4,'fsdp'=8] {'fsdp'}, dimensions={1} | all-to-all | bytes 7340032 | tf_op jit(solution)/shard_map/all_to_all | solution.py:23
  214.6 0.0 all-gather.4.cloned.1.call-update
  214.6 26.1 %copy.27 = bf16[1,4096,1792]{2,0,1:T(2,128)(2,1)} copy(bf16[1,4096,1792]{2,1,0:T(8,128)(2,1)} %param.6) | data formatting | bytes 29360128 | tf_op args[0]
  240.7 147.2 %reduce.1 = bf16[4096,1792]{1,0:T(8,128)(2,1)} reduce(bf16[4096,1,1792]{2,1,0:T(2,128)(2,1)} %bitcast.34, bf16[]{:T(256)} %broadcast.39), dimensions={1}, to_apply=%bitcast.25.reduce_sub_computation | reduce | bytes 29360130
  387.9 11.5 %reshape.41 = bf16[4,2,917504]{2,1,0:T(2,128)(2,1)} reshape(bf16[4096,1792]{1,0:T(8,128)(2,1)} %reduce.1) | data formatting | bytes 29360128
  399.4 7.0 all-to-all-start.2
  406.4 160.1 %all-to-all-done.2 = bf16[4,2,917504]{2,1,0:T(2,128)(2,1)} async-done(((bf16[4,2,917504]{2,1,0:T(2,128)(2,1)}), bf16[4,2,917504]{2,1,0:T(2,128)(2,1)}, u32[]{:S(2)}, u32[]{:S(2)}) %all-to-all-start.2) | async-done | bytes 14680096 | tf_op jit(solution)/shard_map/all_to_all | solution.py:26
  566.5 32.3 %reshape.42 = bf16[4096,1,1792]{2,1,0:T(2,128)(2,1)} reshape(bf16[4,2,917504]{2,1,0:T(2,128)(2,1)} %all-to-all-done.2) | data formatting | bytes 29360128
  598.7 17.6 %copy.23 = bf16[1,4096,1792]{2,1,0:T(8,128)(2,1)} copy(bf16[1,4096,1792]{2,0,1:T(2,128)(2,1)} %bitcast.35) | data formatting | bytes 29360128
  616.4 0.0 all-gather.6.cloned.1.call-done
  616.4 0.0 all-gather.4.cloned.1.call-done
  616.4 113.5 %while.13 = (s32[]{:T(128)}, f32[1024,1792]{1,0:T(8,128)}, f32[1024,1792]{1,0:T(8,128)}, bf16[4,1024,1024]{1,2,0:T(8,128)(2,1)}, bf16[4,1024,1792]{2,1,0:T(8,128...) while((s32[]{:T(128)}, f32[1024,1792]{1,0:T(8,128)}, f32[1024,1792]{1,0:T(8,128)}, ...), condition=%wide.region_2.3_spmd.clone, body=%wide.region_0.2_spmd.clone.sunk | while | flops 3778281472 | bytes 77594760 | solution.py:40
  616.4 1.8 constant_dynamic-slice_fusion.4
  618.1 2.6 copy.29
  620.7 0.0 copy-start
  620.7 2.4 constant_dynamic-slice_fusion.5
  623.1 0.3 copy-done
  623.4 8.0 %multiply_reduce_fusion.2 = f32[1024,1792]{1,0:T(8,128)} fusion(bf16[2,512,1024]{2,1,0:T(8,128)(2,1)S(1)} %bitcast.38, bf16[2,512,1792]{2,1,0:T(8,128)(2,1)S(1)} %bitcast.36), kind=kOutput, calls=%fused_computation.clone.1 | convolution fusion | flops 3763601408 | bytes 13107200 | tf_op jit(solution)/shard_map/while/body/eval_jaxpr/str,stf->srf/dot_general | solution.py:16
  631.4 8.7 %select_add_fusion.2 = (f32[1024,1792]{1,0:T(8,128)}, f32[1024,1792]{1,0:T(8,128)}) fusion(f32[1024,1792]{1,0:T(8,128)} %get-tuple-element.144, f32[1024,1792]{1,0:T(8,128)} %multiply_reduce_fusion.2, pred[]{:T(512)S(6)} %compare.3, bf16[4,1024,1792]{2,1,0:T(8,128)(2,1)} %get-tuple-element.155, s32[]{:T(128)} %get-tuple-element.142, ...), kind=kLoop, calls=%fused_computation.3.clone.1 | loop fusion | flops 14680064 | bytes 40370180 | tf_op jit(solution)/shard_map/while/body/eval_jaxpr/add | solution.py:34
  640.1 1.8 constant_dynamic-slice_fusion.4
  641.8 2.6 copy.29
  644.4 0.0 copy-start
  644.4 2.4 constant_dynamic-slice_fusion.5
  646.8 0.3 copy-done
  647.1 8.0 %multiply_reduce_fusion.2 = f32[1024,1792]{1,0:T(8,128)} fusion(bf16[2,512,1024]{2,1,0:T(8,128)(2,1)S(1)} %bitcast.38, bf16[2,512,1792]{2,1,0:T(8,128)(2,1)S(1)} %bitcast.36), kind=kOutput, calls=%fused_computation.clone.1 | convolution fusion | flops 3763601408 | bytes 13107200 | tf_op jit(solution)/shard_map/while/body/eval_jaxpr/str,stf->srf/dot_general | solution.py:16
  655.1 14.9 %select_add_fusion.2 = (f32[1024,1792]{1,0:T(8,128)}, f32[1024,1792]{1,0:T(8,128)}) fusion(f32[1024,1792]{1,0:T(8,128)} %get-tuple-element.144, f32[1024,1792]{1,0:T(8,128)} %multiply_reduce_fusion.2, pred[]{:T(512)S(6)} %compare.3, bf16[4,1024,1792]{2,1,0:T(8,128)(2,1)} %get-tuple-element.155, s32[]{:T(128)} %get-tuple-element.142, ...), kind=kLoop, calls=%fused_computation.3.clone.1 | loop fusion | flops 14680064 | bytes 40370180 | tf_op jit(solution)/shard_map/while/body/eval_jaxpr/add | solution.py:34
  670.0 1.8 constant_dynamic-slice_fusion.4
  671.7 2.6 copy.29
  674.3 0.0 copy-start
  674.3 2.4 constant_dynamic-slice_fusion.5
  676.7 0.3 copy-done
  677.0 8.0 %multiply_reduce_fusion.2 = f32[1024,1792]{1,0:T(8,128)} fusion(bf16[2,512,1024]{2,1,0:T(8,128)(2,1)S(1)} %bitcast.38, bf16[2,512,1792]{2,1,0:T(8,128)(2,1)S(1)} %bitcast.36), kind=kOutput, calls=%fused_computation.clone.1 | convolution fusion | flops 3763601408 | bytes 13107200 | tf_op jit(solution)/shard_map/while/body/eval_jaxpr/str,stf->srf/dot_general | solution.py:16
  685.0 14.9 %select_add_fusion.2 = (f32[1024,1792]{1,0:T(8,128)}, f32[1024,1792]{1,0:T(8,128)}) fusion(f32[1024,1792]{1,0:T(8,128)} %get-tuple-element.144, f32[1024,1792]{1,0:T(8,128)} %multiply_reduce_fusion.2, pred[]{:T(512)S(6)} %compare.3, bf16[4,1024,1792]{2,1,0:T(8,128)(2,1)} %get-tuple-element.155, s32[]{:T(128)} %get-tuple-element.142, ...), kind=kLoop, calls=%fused_computation.3.clone.1 | loop fusion | flops 14680064 | bytes 40370180 | tf_op jit(solution)/shard_map/while/body/eval_jaxpr/add | solution.py:34
  699.9 1.8 constant_dynamic-slice_fusion.4
  701.7 2.6 copy.29
  704.2 0.0 copy-start
  704.2 2.4 constant_dynamic-slice_fusion.5
  706.6 0.3 copy-done
  706.9 8.0 %multiply_reduce_fusion.2 = f32[1024,1792]{1,0:T(8,128)} fusion(bf16[2,512,1024]{2,1,0:T(8,128)(2,1)S(1)} %bitcast.38, bf16[2,512,1792]{2,1,0:T(8,128)(2,1)S(1)} %bitcast.36), kind=kOutput, calls=%fused_computation.clone.1 | convolution fusion | flops 3763601408 | bytes 13107200 | tf_op jit(solution)/shard_map/while/body/eval_jaxpr/str,stf->srf/dot_general | solution.py:16
  714.9 14.9 %select_add_fusion.2 = (f32[1024,1792]{1,0:T(8,128)}, f32[1024,1792]{1,0:T(8,128)}) fusion(f32[1024,1792]{1,0:T(8,128)} %get-tuple-element.144, f32[1024,1792]{1,0:T(8,128)} %multiply_reduce_fusion.2, pred[]{:T(512)S(6)} %compare.3, bf16[4,1024,1792]{2,1,0:T(8,128)(2,1)} %get-tuple-element.155, s32[]{:T(128)} %get-tuple-element.142, ...), kind=kLoop, calls=%fused_computation.3.clone.1 | loop fusion | flops 14680064 | bytes 40370180 | tf_op jit(solution)/shard_map/while/body/eval_jaxpr/add | solution.py:34
  729.8 8.0 %divide_convert_fusion = bf16[1024,1792]{1,0:T(8,128)(2,1)} fusion(f32[1024,1792]{1,0:T(8,128)} %get-tuple-element.38, f32[1024,1792]{1,0:T(8,128)} %get-tuple-element.39), kind=kLoop, calls=%fused_computation.7 | loop fusion | flops 3670016 | bytes 18350080 | tf_op jit(solution)/shard_map/convert_element_type | solution.py:43
  (3 shorter events, 0.0 us)
Async XLA Ops:
  6.5 609.8 %all-gather.6.cloned.1.call-start = ((), (), s32[]{:S(2)}) async-start(), calls=%async_computation.4 | async-start | bytes 9437184 | tf_op jit(solution)/shard_map/all_gather | solution.py:25
  53.9 5.0 copy-start.1
  56.0 560.3 %all-gather.4.cloned.1.call-start = ((), (), s32[]{:S(2)}) async-start(), calls=%async_computation.3 | async-start | bytes 18350080 | tf_op jit(solution)/shard_map/all_gather | solution.py:27
  399.4 167.1 %all-to-all-start.2 = ((bf16[4,2,917504]{2,1,0:T(2,128)(2,1)}), bf16[4,2,917504]{2,1,0:T(2,128)(2,1)}, u32[]{:S(2)}, u32[]{:S(2)}) async-start(bf16[4,2,917504]{2,1,0:T(2,128)(2,1)} %reshape.41), calls=%async_computation.2 | async-start | bytes 29360128 | tf_op jit(solution)/shard_map/all_to_all | solution.py:26
  620.7 2.7 copy-start
  644.4 2.7 copy-start
  674.3 2.7 copy-start
  704.2 2.7 copy-start
Sparse Core Ops, SparseCore 0:
  56.2 154.8 all-gather.5
  214.7 137.8 all-gather.3
where the time goes:
time: 746 us; the launch traced here: 745 us
  other arithmetic  232 us (31%)
  blocking collectives  174 us (23%)
  waiting for transfers between devices  160 us (21%)
  local copies, waits for them, and re-layouts  126 us (17%)
  matrix products  32 us (4%)
  between operations  13.5 us (2%)
    unnamed x4, other arithmetic  170 us
    all_to_all x1, waiting for transfers between devices, per_device(): lax.all_to_all(weights, 'mp', split_axis=1, concat_axis=0, tiled=True)  160 us
    all_to_all x1, blocking collectives, per_device(): lax.all_to_all(masked, 'fsdp', split_axis=1, concat_axis=0, tiled=True)  154 us
    unnamed x12, local copies, waits for them, and re-layouts  98.3 us
    add x4, other arithmetic, add_model(): denominator + importance  53.4 us
    dot_general x4, matrix products, sequence_fisher(): jnp.einsum('str,stf->srf', acts_split, grads_split, preferred_element_typ...  32 us
    dynamic_slice x12, local copies, waits for them, and re-layouts, per_device(): lax.scan(add_model, start, (acts_models, grads_models, weight_models))  27 us
    all_to_all x1, blocking collectives, per_device(): lax.all_to_all(acts, 'mp', split_axis=2, concat_axis=0, tiled=True)  19.1 us
  transfers between devices with their start and end apart: 3, of which 1 were waited for; matrix products, arithmetic and copies ran while one was open for 32% of the time, Pallas kernels for 0%

commit v1 on v0

v1 whole, which is shorter than its diff:
```python
import functools

import jax
import jax.numpy as jnp
from jax import lax
from jax.experimental import pallas as pl
from jax.experimental.pallas import tpu as pltpu
from jax.sharding import PartitionSpec as P

SEQS = 2
EARLY = 2


damping = 0.1


def remote(src, dst, send_sem, recv_sem, device):
    return pltpu.make_async_remote_copy(
        src_ref=src,
        dst_ref=dst,
        send_sem=send_sem,
        recv_sem=recv_sem,
        device_id=device,
        device_id_type=pl.DeviceIdType.MESH,
    )


def kernel(
    nm, nf, chunk, tile,
    w_ref, a_ref, g_ref, out_ref,
    acts, grads, wbuf, turned, obuf,
    am_send, am_recv, az_send, az_recv, as_send, as_recv,
    gf_send, gf_recv, gm_send, gm_recv, gr_send, w_send, w_recv, local_sem, out_sem,
):
    me, mine = lax.axis_index("mp"), lax.axis_index("fsdp")
    tok, cols = a_ref.shape[0], w_ref.shape[1]
    rows = w_ref.shape[0] // nm
    chunks = rows // chunk
    seq = nf * tok // SEQS
    sibling = mine + 1 - 2 * (mine % 2)
    relayed = nm == 4
    across, up = me + 1 - 2 * (me % 2), me + 2 - 4 * (me // 2)

    def model(d):
        return lax.rem(me + d, nm)

    def peer(d):
        return lax.rem(mine + d, nf)

    def tokens(f):
        return pl.ds(pl.multiple_of(f * tok, tok), tok)

    def acts_part(f):
        return acts.at[:, tokens(f), :]

    def grads_part(m, f):
        return grads.at[m, tokens(f), :]

    own = [
        pltpu.make_async_copy(
            a_ref.at[:, pl.ds(pl.multiple_of(me * rows, rows), rows)],
            acts.at[me, tokens(mine), :], local_sem.at[0]),
        pltpu.make_async_copy(
            g_ref.at[:, pl.ds(pl.multiple_of(mine * cols, cols), cols)],
            grads_part(me, mine), local_sem.at[1]),
        pltpu.make_async_copy(
            w_ref.at[pl.ds(pl.multiple_of(me * rows, rows), rows), :],
            wbuf.at[me], local_sem.at[2]),
    ]
    for copy in own:
        copy.start()

    barrier = pltpu.get_barrier_semaphore()
    for d in range(1, nm):
        pl.semaphore_signal(barrier, inc=1, device_id=(model(d), mine), device_id_type=pl.DeviceIdType.MESH)
    for d in range(1, nf):
        pl.semaphore_signal(barrier, inc=1, device_id=(me, peer(d)), device_id_type=pl.DeviceIdType.MESH)
    pl.semaphore_wait(barrier, nm + nf - 2)

    sent = []

    def start(copy):
        copy.start()
        sent.append(copy)

    for d in range(1, nm):
        j = model(d)
        start(remote(
            a_ref.at[:, pl.ds(pl.multiple_of(j * rows, rows), rows)],
            acts.at[me, tokens(mine), :], am_send.at[d], am_recv.at[me], (j, mine)))
    for d in range(1, nf):
        f = peer(d)
        start(remote(
            g_ref.at[:, pl.ds(pl.multiple_of(f * cols, cols), cols)],
            grads_part(me, mine), gf_send.at[d], gf_recv.at[mine], (me, f)))

    def send_weights(k):
        for d in range(1, nm):
            j = model(d)
            start(remote(
                w_ref.at[pl.ds(pl.multiple_of(j * rows + k * chunk, chunk), chunk), :],
                wbuf.at[me, pl.ds(k * chunk, chunk), :], w_send.at[d, k], w_recv.at[me, k], (j, mine)))

    for k in range(min(EARLY, chunks)):
        send_weights(k)

    def spread(f):
        part = grads_part(me, f)
        if relayed:
            start(remote(part, part, gm_send.at[0, f], gm_recv.at[me, f], (across, mine)))
            start(remote(part, part, gm_send.at[1, f], gm_recv.at[me, f], (up, mine)))
        else:
            for d in range(1, nm):
                start(remote(part, part, gm_send.at[d, f], gm_recv.at[me, f], (model(d), mine)))

    def arrived(m, f):
        part = grads_part(m, f)
        remote(part, part, gm_send.at[0, f], gm_recv.at[m, f], (m, mine)).wait_recv()

    def relay(f):
        odd = f % 2
        source = odd * up + (1 - odd) * across
        target = odd * across + (1 - odd) * up
        arrived(source, f)
        part = grads_part(source, f)
        start(remote(part, part, gr_send.at[f], gm_recv.at[source, f], (target, mine)))

    own[1].wait()
    spread(mine)

    own[0].wait()
    for d in range(1, nm):
        m = model(d)
        part = acts.at[m, tokens(mine), :]
        remote(part, part, am_send.at[d], am_recv.at[m], (m, mine)).wait_recv()
    start(remote(acts_part(mine), acts_part(mine), as_send.at[0], as_recv.at[mine], (me, sibling)))
    for d in range(1, nf // 2):
        start(remote(acts_part(mine), acts_part(mine), az_send.at[d], az_recv.at[mine], (me, peer(2 * d))))

    order = [nf - d for d in range(1, nf)]
    previous = mine
    for d in order:
        f = peer(d)
        part = grads_part(me, f)
        remote(part, part, gf_send.at[d], gf_recv.at[f], (me, f)).wait_recv()
        spread(f)
        if relayed:
            relay(previous)
        previous = f
    if relayed:
        relay(previous)

    for k in range(min(EARLY, chunks), chunks):
        send_weights(k)

    for d in range(1, nf // 2):
        f = lax.rem(mine + nf - 2 * d, nf)
        part = acts_part(f)
        remote(part, part, az_send.at[d], az_recv.at[f], (me, f)).wait_recv()
        start(remote(part, part, as_send.at[d], as_recv.at[f], (me, sibling)))
    for d in range(nf // 2):
        f = lax.rem(sibling + 2 * d, nf)
        part = acts_part(f)
        remote(part, part, as_send.at[d], as_recv.at[f], (me, sibling)).wait_recv()

    for d in range(nf):
        f = peer(d)
        if relayed:
            odd = f % 2
            arrived(odd * across + (1 - odd) * up, f)
            arrived(nm - 1 - me, f)
        else:
            for e in range(1, nm):
                arrived(model(e), f)
    own[2].wait()

    outs = []
    for k in range(chunks):
        here = pl.ds(k * chunk, chunk)
        for m in range(nm):
            turned[m] = acts[m, :, k * chunk:(k + 1) * chunk].T
        for d in range(1, nm):
            m = model(d)
            part = wbuf.at[m, here, :]
            remote(part, part, w_send.at[d, k], w_recv.at[m, k], (m, mine)).wait_recv()
        if k >= 2:
            outs[k - 2].wait()
        slot = k % 2

        @pl.loop(0, cols // tile)
        def _(c):
            span = pl.ds(pl.multiple_of(c * tile, tile), tile)
            numerator = jnp.zeros((chunk, tile), jnp.float32)
            denominator = jnp.zeros((chunk, tile), jnp.float32)
            for m in range(nm):
                fisher = jnp.zeros((chunk, tile), jnp.float32)
                for s in range(SEQS):
                    g = jnp.dot(
                        turned[m, :, s * seq:(s + 1) * seq],
                        grads[m, s * seq:(s + 1) * seq, span],
                        preferred_element_type=jnp.float32)
                    fisher = fisher + g * g
                importance = fisher / SEQS + damping
                numerator = numerator + importance * wbuf[m, here, span].astype(jnp.float32)
                denominator = denominator + importance
            obuf[slot, :, span] = (numerator / denominator).astype(jnp.bfloat16)

        copy = pltpu.make_async_copy(obuf.at[slot], out_ref.at[here, :], out_sem.at[slot])
        copy.start()
        outs.append(copy)
    for copy in outs[-2:]:
        copy.wait()
    for copy in sent:
        copy.wait_send()


def fit(size, most, unit):
    return max(t for t in range(unit, most + 1, unit) if size % t == 0)


def per_device(nm, nf, weights, acts, cotangent, token_ids):
    live_rows = (token_ids[0] > 0).astype(jnp.bfloat16)
    masked = acts[0] * live_rows[:, None]
    _, depth, cols = weights.shape
    rows, tok = depth // nm, acts.shape[1]
    chunk, tile = fit(rows, 256, 16), fit(cols, 256, 128)
    chunks = rows // chunk
    dma = pltpu.SemaphoreType.DMA
    bf16 = jnp.bfloat16
    return pl.pallas_call(
        functools.partial(kernel, nm, nf, chunk, tile),
        out_shape=jax.ShapeDtypeStruct((rows, cols), bf16),
        in_specs=[pl.BlockSpec(memory_space=pl.ANY)] * 3,
        out_specs=pl.BlockSpec(memory_space=pl.ANY),
        scratch_shapes=[
            pltpu.VMEM((nm, nf * tok, rows), bf16),
            pltpu.VMEM((nm, nf * tok, cols), bf16),
            pltpu.VMEM((nm, rows, cols), bf16),
            pltpu.VMEM((nm, chunk, nf * tok), bf16),
            pltpu.VMEM((2, chunk, cols), bf16),
            dma((nm,)), dma((nm,)),
            dma((nf,)), dma((nf,)), dma((nf,)), dma((nf,)),
            dma((nf,)), dma((nf,)),
            dma((nm, nf)), dma((nm, nf)), dma((nf,)),
            dma((nm, chunks)), dma((nm, chunks)),
            dma((3,)), dma((2,)),
        ],
        compiler_params=pltpu.CompilerParams(
            collective_id=0, has_side_effects=True, vmem_limit_bytes=58 * 1024 * 1024
        ),
        cost_estimate=pl.CostEstimate(
            flops=2 * nm * nf * tok * rows * cols,
            bytes_accessed=2 * (depth * cols + tok * depth + nf * tok * cols + rows * cols),
            transcendentals=0),
    )(weights[0], masked, cotangent[0])


def solution(mesh):
    return jax.shard_map(
        functools.partial(per_device, mesh.shape["mp"], mesh.shape["fsdp"]),
        mesh=mesh,
        in_specs=(
            P("mp", None, "fsdp"),
            P("mp", "fsdp", None),
            P("mp", "fsdp", None),
            P("mp", "fsdp"),
        ),
        out_specs=P("mp", "fsdp"),
        check_vma=False,
    )
```

time: 746 us -> 310 us (0.42)
  Pallas kernels: 0 us -> 303 us
  other arithmetic: 232 us -> 2.99 us
  blocking collectives: 174 us -> 0 us
  waiting for transfers between devices: 160 us -> 0 us
  local copies, waits for them, and re-layouts: 126 us -> 4.11 us
  matrix products: 32 us -> 0 us
  between operations: 13.5 us -> 0.01 us
    pallas_call x0 -> x1, Pallas kernels: none -> 303 us  [per_device(): pl.pallas_call(functools.partial(kernel, nm, nf, chunk, tile), out_shape=...]
    all_to_all x2 -> x0, blocking collectives: 174 us -> none  [the longest x1 154 us: per_device(): lax.all_to_all(masked, 'fsdp', split_axis=1, concat_axis=0, tiled=True)]
    unnamed x4 -> x0, other arithmetic: 170 us -> none
    all_to_all x1 -> x0, waiting for transfers between devices: 160 us -> none  [per_device(): lax.all_to_all(weights, 'mp', split_axis=1, concat_axis=0, tiled=True)]
    unnamed x12 -> x1, local copies, waits for them, and re-layouts: 98.3 us -> 4.11 us
    add x4 -> x0, other arithmetic: 53.4 us -> none  [add_model(): denominator + importance]
    dot_general x4 -> x0, matrix products: 32 us -> none  [sequence_fisher(): jnp.einsum('str,stf->srf', acts_split, grads_split, preferred_element_typ...]
    dynamic_slice x12 -> x0, local copies, waits for them, and re-layouts: 27 us -> none  [per_device(): lax.scan(add_model, start, (acts_models, grads_models, weight_models))]
  transfers between devices with their start and end apart: 3 -> 0, of which waited for: 1 -> 0; matrix products, arithmetic and copies ran while one was open for 32% -> 0% of each run, Pallas kernels for 0% -> 0%
where the time goes in v1:
time: 310 us
  Pallas kernels  303 us (98%)
  local copies, waits for them, and re-layouts  4.11 us (1%)
    pallas_call x1, Pallas kernels, per_device(): pl.pallas_call(functools.partial(kernel, nm, nf, chunk, tile), out_shape=...  303 us

profile of v1, /device:TPU:0, one launch (start us, length us, event | category | flops | bytes accessed | tf_op | source)
XLA Modules:
  0.0 310.0 jit_solution(10206315476319013964)
XLA Ops:
  0.0 0.7 fusion
  0.7 2.3 bitcast_multiply_fusion.a_ref
  3.0 302.9 %shard_map.46 = bf16[1024,1792]{1,0:T(8,128)(2,1)} custom-call(bf16[4096,1792]{1,0:T(8,128)(2,1)} %bitcast.6, bf16[128,4096]{1,0:T(8,128)(2,1)} %bitcast_multiply_fusion.a_ref, bf16[128,14336]{1,0:T(8,128)(2,1)} %bitcast.7), custom_call_target="tpu_custom_call" | custom-call | flops 15032385536 | bytes 23068672 | tf_op jit(solution)/shard_map/pallas_call | solution.py:230
  305.9 4.1 %copy.6 = bf16[1024,1792]{1,0:T(8,128)(2,1)} copy(bf16[1024,1792]{1,0:T(8,128)(2,1)} %shard_map.46) | data formatting | bytes 7340032
